TPU v7x, 256 devices: a whole 4x4x8 slice. The times are simulated.
256 devices in a mesh: row: 16 (over y_hi, z), col: 16 (over x, y_lo, core).
Axes of the slice: x: 4, y: 4 (y_hi: 2, y_lo: 2; y = y_hi * 2 + y_lo), z: 8, core: 2. Of those that a mesh axis runs over, the one named last changes fastest.
Arguments:
- template_pair: bfloat16 [2, 64, 1280, 1280], P(None, None, ('row', 'col')), may hold values from -6 to 6
- pair_mask: int32 [1280, 1280], P(('row', 'col')), may hold values 0 or 1
- template_mask: int32 [2, 1280], replicated, may hold values 0 or 1
- in_gain: float32 [64], replicated, may hold values from 0.1 to 1.9
- proj_weight: bfloat16 [64, 256], replicated, may hold values from -0.75 to 0.75
- gate_weight: bfloat16 [64, 64], replicated, may hold values from -0.75 to 0.75
- mid_gain: float32 [64], replicated, may hold values from 0.1 to 1.9
- out_weight: bfloat16 [64, 64], replicated, may hold values from -0.75 to 0.75
- trans_gain: float32 [64], replicated, may hold values from 0.1 to 1.9
- up_weight: bfloat16 [64, 128], replicated, may hold values from -0.75 to 0.75
- down_weight: bfloat16 [128, 64], replicated, may hold values from -0.5 to 0.5
- final_gain: float32 [64], replicated, may hold values from 0.1 to 1.9
- embed_weight: bfloat16 [64, 128], replicated, may hold values from -0.75 to 0.75
Outputs:
- pair_update: bfloat16 [1280, 1280, 128], P(('row', 'col'))
All inputs are finite; a program needn't handle non-finite values. No bound on the sum of `pair_mask` on one device may be relied on, other than what follows from the above.
Results may differ from a plain program's by a relative error of at most 0.0063.
Values may be sent and summed in bfloat16 or wider, within the bound.
A program may use at most 128 MiB of HBM per device.

v0:
```python
import jax
import jax.numpy as jnp
from jax import lax
from jax.sharding import PartitionSpec as P

EPSILON = 1e-05


def channel_norm(values, gain_vector):
    centre = values - jnp.mean(values, axis=1, keepdims=True)
    spread = jnp.mean(centre * centre, axis=1, keepdims=True)
    return centre * lax.rsqrt(spread + EPSILON) * gain_vector[None, :, None, None]


def linear_map(values, weight):
    return jnp.einsum("tcrl,ce->terl", values, weight, preferred_element_type=jnp.float32)


def outer_sum(left_part, block_rows):
    return jnp.einsum(
        "tcik,tcjk->tcij", left_part, block_rows, preferred_element_type=jnp.float32
    ).astype(jnp.bfloat16)


def local(
    template_pair,
    pair_mask,
    template_mask,
    in_gain,
    proj_weight,
    gate_weight,
    mid_gain,
    out_weight,
    trans_gain,
    up_weight,
    down_weight,
    final_gain,
    embed_weight,
):
    channels = template_pair.shape[1]
    own_rows = template_pair.shape[2]
    pair_wide = template_pair.astype(jnp.float32)
    normed = channel_norm(pair_wide, in_gain).astype(jnp.bfloat16)
    projected = linear_map(normed, proj_weight)
    pair_weight = pair_mask.astype(jnp.float32)[None, None]
    left_side = (
        jax.nn.sigmoid(projected[:, channels : 2 * channels])
        * projected[:, :channels]
        * pair_weight
    ).astype(jnp.bfloat16)
    right_side = (
        jax.nn.sigmoid(projected[:, 3 * channels :])
        * projected[:, 2 * channels : 3 * channels]
        * pair_weight
    ).astype(jnp.bfloat16)
    gate_value = jax.nn.sigmoid(linear_map(normed, gate_weight))
    left_moved, right_moved = (
        lax.all_to_all(left_side, "col", split_axis=1, concat_axis=2, tiled=True),
        lax.all_to_all(right_side, "col", split_axis=1, concat_axis=2, tiled=True),
    )
    triangle = outer_sum(left_moved, lax.all_gather(right_moved, "row", axis=2, tiled=True))
    returned = lax.all_to_all(triangle, "col", split_axis=2, concat_axis=1, tiled=True)
    tri_normed = channel_norm(returned.astype(jnp.float32), mid_gain).astype(jnp.bfloat16)
    updated = pair_wide + gate_value * linear_map(tri_normed, out_weight)
    trans_in = channel_norm(updated, trans_gain).astype(jnp.bfloat16)
    hidden = jax.nn.relu(linear_map(trans_in, up_weight)).astype(jnp.bfloat16)
    stacked = updated + linear_map(hidden, down_weight)
    final = channel_norm(stacked, final_gain)
    mask_values = template_mask.astype(jnp.float32)
    first_row = (lax.axis_index("row") * lax.axis_size("col") + lax.axis_index("col")) * own_rows
    own_mask = lax.dynamic_slice_in_dim(mask_values, first_row, own_rows, 1)
    coverage = own_mask[:, :, None] * mask_values[:, None, :]
    counted = jnp.maximum(jnp.sum(coverage, axis=0), 1.0)
    averaged = jnp.sum(coverage[:, None] * final, axis=0) / counted[None]
    activated = jax.nn.relu(averaged).astype(jnp.bfloat16)
    return jnp.einsum(
        "crl,cp->rlp", activated, embed_weight, preferred_element_type=jnp.float32
    ).astype(jnp.bfloat16)


def solution(mesh):
    return jax.shard_map(
        local,
        mesh=mesh,
        in_specs=(
            P(None, None, ("row", "col"), None),
            P(("row", "col"), None),
            P(),
            P(),
            P(),
            P(),
            P(),
            P(),
            P(),
            P(),
            P(),
            P(),
            P(),
        ),
        out_specs=P(("row", "col"), None, None),
        check_vma=False,
    )
```

profile of v0, /device:TPU:1, one launch (start us, length us, event | category | flops | bytes accessed | tf_op | source)
XLA Modules:
  0.0 462.2 jit_solution(6284162494584401806)
XLA Ops:
  6.5 0.0 copy-start
  6.5 0.0 copy-start.3
  6.5 0.0 copy-start.6
  6.5 0.0 copy-start.10
  6.5 0.0 all-gather.2.cloned.1.call-start
  6.6 1.9 convert_reduce_fusion
  8.5 1.9 fusion.8
  10.4 0.0 copy-done.6
  10.5 0.0 copy-done
  10.5 0.0 copy-done.3
  10.5 0.0 copy-done.10
  10.5 1.9 convolution_bitcast_fusion
  12.4 1.9 fusion.17
  14.3 1.7 copy.71
  16.0 29.2 %all_to_all.45 = bf16[2,64,5,1280]{3,0,2,1:T(2,128)(2,1)S(1)} all-to-all(bf16[2,64,5,1280]{3,0,2,1:T(2,128)(2,1)S(1)} %copy.71), channel_id=1, replica_groups=mesh['row'=16,'col'=16] {'col'}, dimensions={1} | all-to-all | bytes 3276800 | tf_op jit(solution)/shard_map/all_to_all | solution.py:59
  45.2 0.6 copy.72
  45.8 1.3 copy.73
  47.1 0.0 all-gather.2.cloned.1.call-update
  47.2 1.7 copy.69
  48.9 25.4 %all_to_all.46 = bf16[2,64,5,1280]{3,0,2,1:T(2,128)(2,1)S(1)} all-to-all(bf16[2,64,5,1280]{3,0,2,1:T(2,128)(2,1)S(1)} %copy.69), channel_id=1, replica_groups=mesh['row'=16,'col'=16] {'col'}, dimensions={1} | all-to-all | bytes 3276800 | tf_op jit(solution)/shard_map/all_to_all | solution.py:58
  74.3 0.6 copy.70
  74.9 313.1 %all-gather.2.cloned.1.call-done = bf16[2,4,1280,1280]{3,2,1,0:T(8,128)(2,1)} async-done(((bf16[2,4,80,1280]{3,2,1,0:T(8,128)(2,1)}), bf16[2,4,1280,1280]{3,2,1,0:T(8,128)(2,1)}) %all-gather.2.cloned.1.call-update) | async-done | bytes 26214416 | tf_op jit(solution)/shard_map/all_gather | solution.py:61
  388.0 14.2 %convolution_convert_fusion.1 = bf16[2,4,80,1280]{3,2,1,0:T(8,128)(2,1)} fusion(bf16[2,4,1280,1280]{3,2,1,0:T(8,128)(2,1)} %all-gather.2.cloned.1.call-done, bf16[2,4,80,1280]{3,1,2,0:T(4,128)(2,1)S(1)} %bitcast.70), kind=kOutput, calls=%fused_computation.43 | convolution fusion | flops 2097971200 | bytes 29491200 | tf_op jit(solution)/shard_map/tcik,tcjk->tcij/dot_general | solution.py:20
  402.2 0.0 copy-start.9
  402.2 0.0 copy-start.13
  402.2 3.5 copy.75
  405.7 5.4 %all-to-all-start.2 = ((bf16[2,4,80,1280]{3,1,0,2:T(4,128)(2,1)}), bf16[2,4,80,1280]{3,1,0,2:T(4,128)(2,1)S(1)}, u32[]{:S(2)}, u32[]{:S(2)}) async-start(bf16[2,4,80,1280]{3,1,0,2:T(4,128)(2,1)} %copy.75), calls=%async_computation.2 | async-start | bytes 3276800 | tf_op jit(solution)/shard_map/all_to_all | solution.py:62
  411.0 0.0 copy-done.9
  411.1 0.1 constant_dynamic-slice_fusion
  411.1 0.0 copy-done.13
  411.1 3.0 fusion.4
  414.1 19.0 %all-to-all-done.2 = bf16[2,4,80,1280]{3,1,0,2:T(4,128)(2,1)S(1)} async-done(((bf16[2,4,80,1280]{3,1,0,2:T(4,128)(2,1)}), bf16[2,4,80,1280]{3,1,0,2:T(4,128)(2,1)S(1)}, u32[]{:S(2)}, u32[]{:S(2)}) %all-to-all-start.2) | async-done | bytes 1638432 | tf_op jit(solution)/shard_map/all_to_all | solution.py:62
  433.1 0.3 copy_convert_fusion
  433.4 2.1 copy.77
  435.5 0.5 reduce_sum.92
  436.0 0.9 multiply_reduce_fusion.3
  437.0 0.0 copy-start.11
  437.0 2.5 copy.78
  439.6 0.0 copy-start.4
  439.6 0.0 copy-start.5
  439.6 0.0 copy-start.7
  439.7 0.0 copy-done.11
  439.7 2.1 fusion.23
  441.8 0.0 copy-done.4
  441.8 0.2 copy-done.5
  442.0 0.0 copy-done.7
  442.0 1.0 fusion.46
  443.0 0.0 copy-start.8
  443.0 0.4 multiply_reduce_fusion.2
  443.5 0.2 copy-done.8
  443.7 6.3 %fusion.47 = (f32[2,5,1280]{2,1,0:T(8,128)S(1)}, f32[2,64,5,1280]{3,1,2,0:T(8,128)}) fusion(f32[2,64,5,1280]{3,1,2,0:T(8,128)S(1)} %get-tuple-element.10, bf16[128,64]{0,1:T(8,128)(2,1)S(1)} %copy-done.8, f32[64]{0:T(128)} %param.21, f32[2,5,1280]{2,1,0:T(8,128)S(1)} %add_rsqrt_fusion.1, f32[2,5,1280]{2,1,0:T(8,128)S(1)} %broadcast_multiply_fusion.1, ...), kind=kOutput, calls=%fused_computation.74 | convolution fusion | flops 427609600 | bytes 6740224 | tf_op jit(solution)/shard_map/tcrl,ce->terl/dot_general | solution.py:16
  450.0 0.0 copy-start.2
  450.0 0.0 copy-start.12
  450.0 2.5 multiply_reduce_fusion.1
  452.5 0.0 copy-start.14
  452.6 0.1 fusion.37
  452.6 0.3 copy-done.2
  452.9 0.0 copy-done.12
  452.9 0.0 copy-start.1
  452.9 0.6 multiply_reduce_fusion
  453.6 0.0 copy-done.14
  453.6 1.8 convolution_convert_fusion
  455.4 0.0 copy-done.1
  (12 shorter events, 0.2 us)
Async XLA Ops:
  6.5 3.9 copy-start
  6.5 3.9 copy-start.3
  6.5 3.9 copy-start.6
  6.5 3.9 copy-start.10
  6.5 381.5 %all-gather.2.cloned.1.call-start = ((), (), s32[]{:S(2)}) async-start(), calls=%async_computation.3 | async-start | bytes 27852800 | tf_op jit(solution)/shard_map/all_gather | solution.py:61
  402.2 8.8 %copy-start.9 = (s32[2,1280]{1,0:T(2,128)S(1)}, s32[2,1280]{1,0:T(2,128)}, u32[]{:S(2)}) copy-start(s32[2,1280]{1,0:T(2,128)} %param.15) | copy-start | bytes 30724
  402.2 8.9 %copy-start.13 = (bf16[64,64]{1,0:T(8,128)(2,1)S(1)}, bf16[64,64]{1,0:T(8,128)(2,1)}, u32[]{:S(2)}) copy-start(bf16[64,64]{1,0:T(8,128)(2,1)} %param.18) | copy-start | bytes 24580
  405.7 27.4 %all-to-all-start.2 = ((bf16[2,4,80,1280]{3,1,0,2:T(4,128)(2,1)}), bf16[2,4,80,1280]{3,1,0,2:T(4,128)(2,1)S(1)}, u32[]{:S(2)}, u32[]{:S(2)}) async-start(bf16[2,4,80,1280]{3,1,0,2:T(4,128)(2,1)} %copy.75), calls=%async_computation.2 | async-start | bytes 3276800 | tf_op jit(solution)/shard_map/all_to_all | solution.py:62
  437.0 2.6 copy-start.11
  439.6 2.3 copy-start.4
  439.6 2.4 copy-start.5
  439.6 2.4 copy-start.7
  443.0 0.7 copy-start.8
  450.0 2.9 copy-start.2
  450.0 2.9 copy-start.12
  452.5 1.0 copy-start.14
  452.9 2.5 copy-start.1
Sparse Core Ops, SparseCore 0:
  47.3 340.6 all-gather.1
where the time goes:
time: 463 us; the launch traced here: 462 us
  waiting for transfers between devices  332 us (72%)
  blocking collectives  54.5 us (12%)
  matrix products  28.2 us (6%)
  local copies, waits for them, and re-layouts  14.9 us (3%)
  between operations  13.7 us (3%)
  other arithmetic  13.4 us (3%)
  starting transfers between devices  5.41 us (1%)
    all_gather x1, waiting for transfers between devices, local(): lax.all_gather(right_moved, 'row', axis=2, tiled=True)  313 us
    all_to_all x1, blocking collectives, local(): lax.all_to_all(right_side, 'col', split_axis=1, concat_axis=2, tiled=True)  29.2 us
    all_to_all x1, blocking collectives, local(): lax.all_to_all(left_side, 'col', split_axis=1, concat_axis=2, tiled=True)  25.4 us
    all_to_all x1, waiting for transfers between devices, local(): lax.all_to_all(triangle, 'col', split_axis=2, concat_axis=1, tiled=True)  19 us
    dot_general x1, matrix products, outer_sum(): jnp.einsum('tcik,tcjk->tcij', left_part, block_rows, preferred_element_ty...  14.2 us
    dot_general x4, matrix products, linear_map(): jnp.einsum('tcrl,ce->terl', values, weight, preferred_element_type=jnp.fl...  12.2 us
  transfers between devices with their start and end apart: 2, of which 2 were waited for; matrix products, arithmetic and copies ran while one was open for 1% of the time, Pallas kernels for 0%

commit v1 on v0

v1 whole, which is shorter than its diff:
```python
import functools

import jax
import jax.numpy as jnp
from jax import lax
from jax.experimental import pallas as pl
from jax.experimental.pallas import tpu as pltpu
from jax.sharding import PartitionSpec as P

EPSILON = 1e-05
MESH = pl.DeviceIdType.MESH
F32, BF16 = jnp.float32, jnp.bfloat16
Z = 8
ROWS = 5
L = 1280
LANES = 256
BLOCKS = L // LANES


def device_at(plane, z, core):
    x, y = plane // 4, lax.rem(plane, 4)
    return ((y // 2) * Z + lax.rem(z + Z, Z), x * 4 + lax.rem(y, 2) * 2 + core)


def column(row_vector):
    n = row_vector.shape[1]
    rows = lax.broadcasted_iota(jnp.int32, (n, n), 0)
    lanes = lax.broadcasted_iota(jnp.int32, (n, n), 1)
    return jnp.sum(jnp.where(rows == lanes, row_vector, 0.0), axis=1, keepdims=True)


def norm(values, gain):
    centre = values - jnp.mean(values, axis=0, keepdims=True)
    spread = jnp.mean(centre * centre, axis=0, keepdims=True)
    return centre * lax.rsqrt(spread + EPSILON) * gain


def dot(a, b):
    return jnp.dot(a, b, preferred_element_type=F32)


def weave(first, second):
    pieces = []
    for g in range(first.shape[0] // 8):
        pieces += [first[8 * g : 8 * g + 8], second[8 * g : 8 * g + 8]]
    return jnp.concatenate(pieces, axis=0)


def unweave(both):
    blocks = both.shape[0] // 8
    return tuple(
        jnp.concatenate([both[8 * b : 8 * b + 8] for b in range(t, blocks, 2)], axis=0)
        for t in range(2)
    )


def whole(ref, sem):
    pltpu.make_async_copy(ref, ref, sem).wait()


def kernel(
    pair,
    pair_mask,
    template_mask,
    in_gain,
    proj_weight,
    gate_weight,
    mid_gain,
    out_weight,
    trans_gain,
    up_weight,
    down_weight,
    final_gain,
    embed_weight,
    result,
    proj_t,
    out_t,
    up_t,
    down_t,
    gains,
    own_mask,
    forth,
    back,
    gate,
    left_sent,
    right_sent,
    left_mid,
    right_mid,
    left_turned,
    right_turned,
    left_held,
    right_held,
    left_flat,
    right_flat,
    right_rows,
    tri_made,
    tri_mid,
    tri_turned,
    tri_held,
    out_held,
    z_left,
    z_right,
    z_tri,
    p_left,
    p_right,
    p_tri,
    across,
    z_out,
    p_out,
    across_out,
    result_sem,
):
    row, col = lax.axis_index("row"), lax.axis_index("col")
    z, core = lax.rem(row, Z), lax.rem(col, 2)
    place = (col // 4) * 4 + (row // Z) * 2 + lax.rem(col // 2, 2)
    device = row * 16 + col
    group = lax.rem(z - core + Z, Z)
    partner = device_at(place, z + 1 - 2 * core, 1 - core)

    barrier = pltpu.get_barrier_semaphore()
    for step in range(1, Z):
        for other in range(2):
            pl.semaphore_signal(
                barrier, inc=1, device_id=device_at(place, z + step, other), device_id_type=MESH
            )
    pl.semaphore_signal(
        barrier, inc=1, device_id=device_at(place, z, 1 - core), device_id_type=MESH
    )

    def greet(step, carry):
        pl.semaphore_signal(
            barrier,
            inc=1,
            device_id=device_at(lax.bitwise_xor(place, step), z, core),
            device_id_type=MESH,
        )
        return carry

    lax.fori_loop(1, 16, greet, 0)

    proj_t[0:256, :] = jnp.transpose(proj_weight[...].astype(F32)).astype(BF16)
    proj_t[256:320, :] = jnp.transpose(gate_weight[...].astype(F32)).astype(BF16)
    out_t[...] = jnp.transpose(out_weight[...].astype(F32)).astype(BF16)
    up_t[...] = jnp.transpose(up_weight[...].astype(F32)).astype(BF16)
    down_t[...] = jnp.transpose(down_weight[...].astype(F32)).astype(BF16)
    for n, vector in enumerate((in_gain, mid_gain, trans_gain, final_gain)):
        gains[n] = column(vector[...])
    lanes = lax.broadcasted_iota(jnp.int32, (2, L), 1)
    for r in range(ROWS):
        own_mask[r] = jnp.sum(
            jnp.where(lanes == device * ROWS + r, template_mask[...].astype(F32), 0.0),
            axis=1,
            keepdims=True,
        )
    at = lax.broadcasted_iota(jnp.int32, (128, 128), 0)
    of = lax.broadcasted_iota(jnp.int32, (128, 128), 1)
    forth[...] = jnp.where(of == (at % 8) * 16 + at // 8, 1.0, 0.0).astype(BF16)
    back[...] = jnp.where(of == (at % 16) * 8 + at // 16, 1.0, 0.0).astype(BF16)

    def make(r):
        for block in range(BLOCKS):
            span = pl.ds(block * LANES, LANES)
            mask = pair_mask[pl.ds(r, 1), span].astype(F32)
            lefts, rights, gates = [], [], []
            for t in range(2):
                normed = norm(pair[t, r, :, span].astype(F32), gains[0]).astype(BF16)
                projected = dot(proj_t[...], normed)
                lefts.append(jax.nn.sigmoid(projected[64:128]) * projected[0:64] * mask)
                rights.append(jax.nn.sigmoid(projected[192:256]) * projected[128:192] * mask)
                gates.append(jax.nn.sigmoid(projected[256:320]))
            right_sent[r, :, span] = weave(*rights).astype(BF16)
            left_sent[r, :, span] = weave(*lefts).astype(BF16)
            gate[r, 0, :, span] = gates[0]
            gate[r, 1, :, span] = gates[1]

    def send_z(r, sent, mid, recv):
        def send(g, slot, where):
            pltpu.make_async_remote_copy(
                sent.at[r, pl.ds(pl.multiple_of(g * 16, 16), 16)],
                mid.at[r, pl.ds(pl.multiple_of(slot * 16, 16), 16)],
                z_out,
                recv.at[r],
                device_id=where,
                device_id_type=MESH,
            ).start()

        for m in (3, 2, 1):
            send(lax.rem(z + m, Z), (3 - m) * 2 + core, device_at(place, z + m, 0))
            send(lax.rem(z + 7 - m, Z), m * 2 + core, device_at(place, z - m, 1))
        send(lax.rem(z + 7 + core, Z), 6 * core + core, device_at(place, z, 1 - core))
        pltpu.make_async_copy(
            sent.at[r, pl.ds(pl.multiple_of(group * 16, 16), 16)],
            mid.at[r, pl.ds(pl.multiple_of((6 - 5 * core) * 16, 16), 16)],
            recv.at[r],
        ).start()

    def send_plane(r, turned, held, recv):
        def send(step, carry):
            other = lax.bitwise_xor(place, step)
            pltpu.make_async_remote_copy(
                turned.at[r, other],
                held.at[r, place],
                p_out,
                recv.at[r],
                device_id=device_at(other, z, core),
                device_id_type=MESH,
            ).start()
            return carry

        lax.fori_loop(1, 16, send, 0)
        pltpu.make_async_copy(turned.at[r, place], held.at[r, place], recv.at[r]).start()

    def turn(r, mid, turned):
        for block in range(BLOCKS):
            span = pl.ds(block * LANES, LANES)
            moved = dot(forth[...], mid[r, :, span])
            turned[r, :, :, span] = moved.reshape(16, 8, LANES).astype(BF16)

    def turn_back(r):
        for block in range(BLOCKS):
            span = pl.ds(block * LANES, LANES)
            value = tri_mid[r, :, :, span].astype(F32).reshape(128, LANES).astype(BF16)
            tri_turned[r, :, span] = dot(back[...], value).astype(BF16)

    def send_back(r):
        def send(slot, where):
            pltpu.make_async_remote_copy(
                tri_turned.at[r, pl.ds(pl.multiple_of(slot * 16, 16), 16)],
                tri_held.at[r, pl.ds(pl.multiple_of(group * 16, 16), 16)],
                z_out,
                z_tri.at[r],
                device_id=where,
                device_id_type=MESH,
            ).start()

        for m in (3, 2, 1):
            for other in range(2):
                slot = ((3 - m) + core * (2 * m - 3)) * 2 + other
                send(slot, device_at(place, z - m + 2 * m * core, other))
        send(7 - 7 * core, device_at(place, z, 1 - core))
        pltpu.make_async_copy(
            tri_turned.at[r, pl.ds(pl.multiple_of((6 - 5 * core) * 16, 16), 16)],
            tri_held.at[r, pl.ds(pl.multiple_of(group * 16, 16), 16)],
            z_tri.at[r],
        ).start()

    def exchange(r):
        return pltpu.make_async_remote_copy(
            right_held.at[core, r],
            right_held.at[core, r],
            across_out,
            across.at[r],
            device_id=partner,
            device_id_type=MESH,
        )

    def send_right(r, carry):
        make(r)

        @pl.when(r == 0)
        def _():
            pl.semaphore_wait(barrier, 30)

        send_z(r, right_sent, right_mid, z_right)
        return carry

    def pass_right(r, carry):
        send_z(r, left_sent, left_mid, z_left)
        whole(right_mid.at[r], z_right.at[r])
        turn(r, right_mid, right_turned)
        send_plane(r, right_turned, right_held.at[core], p_right)
        return carry

    def give_right(r, carry):
        whole(right_held.at[core, r], p_right.at[r])
        exchange(r).start()
        return carry

    def pass_left(r, carry):
        whole(left_mid.at[r], z_left.at[r])
        turn(r, left_mid, left_turned)
        send_plane(r, left_turned, left_held, p_left)
        return carry

    def flatten(r, carry):
        whole(right_held.at[1 - core, r], across.at[r])
        for side in range(2):
            for block in range(BLOCKS):
                span = pl.ds(block * LANES, LANES)
                value = right_held[side, r, :, :, span].astype(F32).reshape(128, LANES)
                start = pl.multiple_of((side * ROWS + r) * 128, 128)
                right_flat[pl.ds(start, 128), span] = value.astype(BF16)
        return carry

    def order(block, carry):
        held = lax.broadcasted_iota(jnp.int32, (1, L), 1)
        chunk = held >> 7
        side = jnp.where(chunk >= ROWS, 1, 0)
        r = chunk - ROWS * side
        source = (held >> 3) & 15
        source_z = (group + 5 + ((held >> 1) & 3) + 4 * side) & 7
        x, y = source >> 2, source & 3
        owner = (((y >> 1) * Z + source_z) * 4 + x) * 4 + (y & 1) * 2 + (held & 1)
        natural = owner * ROWS + r
        start = pl.multiple_of(block * LANES, LANES)
        rows = lax.broadcasted_iota(jnp.int32, (LANES, L), 0) + start
        chosen = jnp.where(rows == natural, 1.0, 0.0).astype(BF16)
        for part in range(BLOCKS):
            span = pl.ds(part * LANES, LANES)
            right_rows[pl.ds(start, LANES), span] = dot(chosen, right_flat[:, span]).astype(BF16)
        return carry

    def multiply(r, carry):
        whole(left_held.at[r], p_left.at[r])
        for block in range(BLOCKS):
            span = pl.ds(block * LANES, LANES)
            value = left_held[r, :, :, span].astype(F32).reshape(128, LANES)
            left_flat[:, span] = value.astype(BF16)
        for block in range(BLOCKS):
            span = pl.ds(block * LANES, LANES)
            product = lax.dot_general(
                left_flat[...],
                right_rows[span, :],
                (((1,), (1,)), ((), ())),
                preferred_element_type=F32,
            )
            tri_made[r, :, :, span] = product.reshape(16, 8, LANES).astype(BF16)
        send_plane(r, tri_made, tri_mid, p_tri)
        return carry

    def give_back(r, carry):
        whole(tri_mid.at[r], p_tri.at[r])
        turn_back(r)
        send_back(r)
        return carry

    def finish(r, carry):
        whole(tri_held.at[r], z_tri.at[r])
        for block in range(BLOCKS):
            span = pl.ds(block * LANES, LANES)
            triangles = unweave(tri_held[r, :, span].astype(F32))
            total, counted = 0.0, 0.0
            for t in range(2):
                tri_normed = norm(triangles[t], gains[1]).astype(BF16)
                updated = pair[t, r, :, span].astype(F32) + gate[r, t, :, span] * dot(
                    out_t[...], tri_normed
                )
                trans_in = norm(updated, gains[2]).astype(BF16)
                hidden = jnp.maximum(dot(up_t[...], trans_in), 0.0).astype(BF16)
                stacked = updated + dot(down_t[...], hidden)
                final = norm(stacked, gains[3])
                coverage = own_mask[r, t : t + 1, :] * template_mask[t : t + 1, span].astype(F32)
                total = total + coverage * final
                counted = counted + coverage
            averaged = total / jnp.maximum(counted, 1.0)
            activated = jnp.transpose(jnp.maximum(averaged, 0.0)).astype(BF16)
            out_held[r, span, :] = dot(activated, embed_weight[...]).astype(BF16)
        pltpu.make_async_copy(out_held.at[r], result.at[r], result_sem.at[r]).start()
        return carry

    lax.fori_loop(0, ROWS, send_right, 0)

    def right_step(r, carry):
        pass_right(r, 0)

        @pl.when(r > 0)
        def _():
            give_right(r - 1, 0)

        return carry

    lax.fori_loop(0, ROWS, right_step, 0)
    give_right(ROWS - 1, 0)
    pass_left(0, 0)
    lax.fori_loop(0, ROWS, flatten, 0)
    lax.fori_loop(0, BLOCKS, order, 0)

    def step(s, carry):
        @pl.when(s < ROWS)
        def _():
            pass_left(s, 0)

        multiply(s - 1, 0)

        @pl.when(s > 1)
        def _():
            give_back(s - 2, 0)

        return carry

    lax.fori_loop(1, ROWS + 1, step, 0)
    give_back(ROWS - 1, 0)
    lax.fori_loop(0, ROWS, finish, 0)

    def left_by_now(r, carry):
        for sent in (left_sent, right_sent, tri_turned):
            whole(sent.at[r, pl.ds(0, 112)], z_out)
        for turned in (left_turned, right_turned, tri_made):
            whole(turned.at[r, pl.ds(0, 15)], p_out)
        whole(right_held.at[core, r], across_out)
        pltpu.make_async_copy(out_held.at[r], result.at[r], result_sem.at[r]).wait()
        return carry

    lax.fori_loop(0, ROWS, left_by_now, 0)


def local(template_pair, pair_mask, template_mask, in_gain, proj_weight, gate_weight, mid_gain,
          out_weight, trans_gain, up_weight, down_weight, final_gain, embed_weight):
    flat = (ROWS, 128, L)
    blocks = (ROWS, 16, 8, L)
    dma = pltpu.SemaphoreType.DMA
    vmem = pltpu.VMEM
    return pl.pallas_call(
        kernel,
        out_shape=jax.ShapeDtypeStruct((ROWS, L, 128), BF16),
        in_specs=[pl.BlockSpec(memory_space=pltpu.VMEM)] * 13,
        out_specs=pl.BlockSpec(memory_space=pl.ANY),
        scratch_shapes=[
            vmem((320, 64), BF16),
            vmem((64, 64), BF16),
            vmem((128, 64), BF16),
            vmem((64, 128), BF16),
            vmem((4, 64, 1), F32),
            vmem((ROWS, 2, 1), F32),
            vmem((128, 128), BF16),
            vmem((128, 128), BF16),
            vmem((ROWS, 2, 64, L), F32),
            vmem(flat, BF16),
            vmem(flat, BF16),
            vmem(flat, BF16),
            vmem(flat, BF16),
            vmem(blocks, BF16),
            vmem(blocks, BF16),
            vmem(blocks, BF16),
            vmem((2, *blocks), BF16),
            vmem((128, L), BF16),
            vmem((L, L), BF16),
            vmem((L, L), BF16),
            vmem(blocks, BF16),
            vmem(blocks, BF16),
            vmem(flat, BF16),
            vmem(flat, BF16),
            vmem((ROWS, L, 128), BF16),
            *[dma((ROWS,)) for _ in range(7)],
            dma,
            dma,
            dma,
            dma((ROWS,)),
        ],
        compiler_params=pltpu.CompilerParams(
            collective_id=0, has_side_effects=True, vmem_limit_bytes=60 * 2**20
        ),
    )(
        template_pair.transpose(0, 2, 1, 3),
        pair_mask,
        template_mask,
        in_gain.reshape(1, -1),
        proj_weight,
        gate_weight,
        mid_gain.reshape(1, -1),
        out_weight,
        trans_gain.reshape(1, -1),
        up_weight,
        down_weight,
        final_gain.reshape(1, -1),
        embed_weight,
    )


def solution(mesh):
    return jax.shard_map(
        local,
        mesh=mesh,
        in_specs=(P(None, None, ("row", "col"), None), P(("row", "col"), None), *[P()] * 11),
        out_specs=P(("row", "col"), None, None),
        check_vma=False,
    )
```

time: 463 us -> 150 us (0.32)
  waiting for transfers between devices: 332 us -> 0 us
  Pallas kernels: 0 us -> 145 us
  blocking collectives: 54.5 us -> 0 us
  matrix products: 28.2 us -> 0 us
  between operations: 13.7 us -> 0.01 us
  other arithmetic: 13.4 us -> 0 us
  local copies, waits for them, and re-layouts: 14.9 us -> 4.13 us
  starting transfers between devices: 5.41 us -> 0 us
    all_gather x1 -> x0, waiting for transfers between devices: 313 us -> none  [local(): lax.all_gather(right_moved, 'row', axis=2, tiled=True)]
    pallas_call x0 -> x1, Pallas kernels: none -> 145 us  [local(): pl.pallas_call(kernel, out_shape=jax.ShapeDtypeStruct((ROWS, L, 128), BF1...]
    all_to_all x2 -> x0, blocking collectives: 54.5 us -> none  [the longest x1 29.2 us: local(): lax.all_to_all(right_side, 'col', split_axis=1, concat_axis=2, tiled=True)]
    dot_general x6 -> x0, matrix products: 28.2 us -> none  [the longest x1 14.2 us: outer_sum(): jnp.einsum('tcik,tcjk->tcij', left_part, block_rows, preferred_element_ty...]
    all_to_all x1 -> x0, waiting for transfers between devices: 19 us -> none  [local(): lax.all_to_all(triangle, 'col', split_axis=2, concat_axis=1, tiled=True)]
    convert_element_type x5 -> x0, local copies, waits for them, and re-layouts: 11.5 us -> none  [the longest x2 4.64 us: local(): returned.astype(jnp.float32)]
    reduce_sum x8 -> x0, other arithmetic: 8.89 us -> none  [the longest x4 5.82 us: channel_norm(): spread = jnp.mean(centre * centre, axis=1, keepdims=True)]
    all_to_all x1 -> x0, starting transfers between devices: 5.37 us -> none  [local(): lax.all_to_all(triangle, 'col', split_axis=2, concat_axis=1, tiled=True)]
  transfers between devices with their start and end apart: 2 -> 0, of which waited for: 2 -> 0; matrix products, arithmetic and copies ran while one was open for 1% -> 0% of each run, Pallas kernels for 0% -> 0%
where the time goes in v1:
time: 150 us
  Pallas kernels  145 us (97%)
  local copies, waits for them, and re-layouts  4.13 us (3%)
    pallas_call x1, Pallas kernels, local(): pl.pallas_call(kernel, out_shape=jax.ShapeDtypeStruct((ROWS, L, 128), BF1...  145 us
    unnamed x2, local copies, waits for them, and re-layouts  4.13 us

profile of v1, /device:TPU:1, one launch (start us, length us, event | category | flops | bytes accessed | tf_op | source)
XLA Modules:
  0.0 149.6 jit_solution(14549562808475454385)
XLA Ops:
  0.0 1.4 copy.14.down_weight
  1.4 145.5 %shard_map.127 = bf16[5,1280,128]{2,1,0:T(8,128)(2,1)} custom-call(bf16[2,5,64,1280]{3,2,1,0:T(8,128)(2,1)} %bitcast.5, s32[5,1280]{1,0:T(8,128)} %pair_mask.1, s32[2,1280]{1,0:T(2,128)} %template_mask.1, f32[1,64]{1,0:T(1,128)} %bitcast.6, bf16[64,256]{1,0:T(8,128)(2,1)} %proj_weight.1, bf16[64,64]{1,0:T(8,128)(2,1)} %gate_weight.1, f32[1,64]{1,0:T(1,128)} %bitcast.7, ...), custom_call_target="tpu_custom_call" | custom-call | tf_op jit(solution)/shard_map/pallas_call | solution.py:413
  146.9 2.7 %copy.16 = bf16[5,1280,128]{2,1,0:T(8,128)(2,1)} copy(bf16[5,1280,128]{2,1,0:T(8,128)(2,1)} %shard_map.127) | data formatting | bytes 3276800

commit v2 on v1

--- a/solution.py
+++ b/solution.py
@@ -15,11 +15,12 @@
 L = 1280
 LANES = 256
 BLOCKS = L // LANES
+AHEAD = 2
 
 
 def device_at(plane, z, core):
-    x, y = plane // 4, lax.rem(plane, 4)
-    return ((y // 2) * Z + lax.rem(z + Z, Z), x * 4 + lax.rem(y, 2) * 2 + core)
+    row = ((plane & 2) << 2) + (z & (Z - 1))
+    return (row, (plane & 12) + ((plane & 1) << 1) + core)
 
 
 def column(row_vector):
@@ -30,9 +31,13 @@
 
 
 def norm(values, gain):
-    centre = values - jnp.mean(values, axis=0, keepdims=True)
-    spread = jnp.mean(centre * centre, axis=0, keepdims=True)
+    centre = values - jnp.mean(values, axis=-2, keepdims=True)
+    spread = jnp.mean(centre * centre, axis=-2, keepdims=True)
     return centre * lax.rsqrt(spread + EPSILON) * gain
+
+
+def norm_both(values, gain):
+    return norm(values.reshape(2, 64, -1), gain).reshape(values.shape)
 
 
 def dot(a, b):
@@ -48,10 +53,8 @@
 
 def unweave(both):
     blocks = both.shape[0] // 8
-    return tuple(
-        jnp.concatenate([both[8 * b : 8 * b + 8] for b in range(t, blocks, 2)], axis=0)
-        for t in range(2)
-    )
+    pieces = [both[8 * b : 8 * b + 8] for t in range(2) for b in range(t, blocks, 2)]
+    return jnp.concatenate(pieces, axis=0)
 
 
 def whole(ref, sem):
@@ -71,7 +74,6 @@
     up_weight,
     down_weight,
     final_gain,
-    embed_weight,
     result,
     proj_t,
     out_t,
@@ -91,6 +93,7 @@
     left_held,
     right_held,
     left_flat,
+    tri_flat,
     right_flat,
     right_rows,
     tri_made,
@@ -111,10 +114,10 @@
     result_sem,
 ):
     row, col = lax.axis_index("row"), lax.axis_index("col")
-    z, core = lax.rem(row, Z), lax.rem(col, 2)
-    place = (col // 4) * 4 + (row // Z) * 2 + lax.rem(col // 2, 2)
+    z, core = row & (Z - 1), col & 1
+    place = (col & 12) + ((row & Z) >> 2) + ((col & 2) >> 1)
     device = row * 16 + col
-    group = lax.rem(z - core + Z, Z)
+    group = (z - core) & (Z - 1)
     partner = device_at(place, z + 1 - 2 * core, 1 - core)
 
     barrier = pltpu.get_barrier_semaphore()
@@ -140,9 +143,14 @@
 
     proj_t[0:256, :] = jnp.transpose(proj_weight[...].astype(F32)).astype(BF16)
     proj_t[256:320, :] = jnp.transpose(gate_weight[...].astype(F32)).astype(BF16)
-    out_t[...] = jnp.transpose(out_weight[...].astype(F32)).astype(BF16)
-    up_t[...] = jnp.transpose(up_weight[...].astype(F32)).astype(BF16)
-    down_t[...] = jnp.transpose(down_weight[...].astype(F32)).astype(BF16)
+    out_t[...] = jnp.zeros_like(out_t)
+    up_t[...] = jnp.zeros_like(up_t)
+    down_t[...] = jnp.zeros_like(down_t)
+    for t in range(2):
+        own, wide = pl.ds(64 * t, 64), pl.ds(128 * t, 128)
+        out_t[own, own] = jnp.transpose(out_weight[...].astype(F32)).astype(BF16)
+        up_t[wide, own] = jnp.transpose(up_weight[...].astype(F32)).astype(BF16)
+        down_t[own, wide] = down_weight[...]
     for n, vector in enumerate((in_gain, mid_gain, trans_gain, final_gain)):
         gains[n] = column(vector[...])
     lanes = lax.broadcasted_iota(jnp.int32, (2, L), 1)
@@ -170,8 +178,7 @@
                 gates.append(jax.nn.sigmoid(projected[256:320]))
             right_sent[r, :, span] = weave(*rights).astype(BF16)
             left_sent[r, :, span] = weave(*lefts).astype(BF16)
-            gate[r, 0, :, span] = gates[0]
-            gate[r, 1, :, span] = gates[1]
+            gate[r, :, span] = jnp.concatenate(gates, axis=0)
 
     def send_z(r, sent, mid, recv):
         def send(g, slot, where):
@@ -185,9 +192,9 @@
             ).start()
 
         for m in (3, 2, 1):
-            send(lax.rem(z + m, Z), (3 - m) * 2 + core, device_at(place, z + m, 0))
-            send(lax.rem(z + 7 - m, Z), m * 2 + core, device_at(place, z - m, 1))
-        send(lax.rem(z + 7 + core, Z), 6 * core + core, device_at(place, z, 1 - core))
+            send((z + m) & (Z - 1), (3 - m) * 2 + core, device_at(place, z + m, 0))
+            send((z + 7 - m) & (Z - 1), m * 2 + core, device_at(place, z - m, 1))
+        send((z + 7 + core) & (Z - 1), 6 * core + core, device_at(place, z, 1 - core))
         pltpu.make_async_copy(
             sent.at[r, pl.ds(pl.multiple_of(group * 16, 16), 16)],
             mid.at[r, pl.ds(pl.multiple_of((6 - 5 * core) * 16, 16), 16)],
@@ -265,7 +272,6 @@
         return carry
 
     def pass_right(r, carry):
-        send_z(r, left_sent, left_mid, z_left)
         whole(right_mid.at[r], z_right.at[r])
         turn(r, right_mid, right_turned)
         send_plane(r, right_turned, right_held.at[core], p_right)
@@ -304,10 +310,7 @@
         natural = owner * ROWS + r
         start = pl.multiple_of(block * LANES, LANES)
         rows = lax.broadcasted_iota(jnp.int32, (LANES, L), 0) + start
-        chosen = jnp.where(rows == natural, 1.0, 0.0).astype(BF16)
-        for part in range(BLOCKS):
-            span = pl.ds(part * LANES, LANES)
-            right_rows[pl.ds(start, LANES), span] = dot(chosen, right_flat[:, span]).astype(BF16)
+        right_rows[pl.ds(start, LANES), :] = jnp.where(rows == natural, 1.0, 0.0).astype(BF16)
         return carry
 
     def multiply(r, carry):
@@ -320,11 +323,20 @@
             span = pl.ds(block * LANES, LANES)
             product = lax.dot_general(
                 left_flat[...],
+                right_flat[span, :],
+                (((1,), (1,)), ((), ())),
+                preferred_element_type=F32,
+            )
+            tri_flat[:, span] = product.astype(BF16)
+        for block in range(BLOCKS):
+            span = pl.ds(block * LANES, LANES)
+            moved = lax.dot_general(
+                tri_flat[...],
                 right_rows[span, :],
                 (((1,), (1,)), ((), ())),
                 preferred_element_type=F32,
             )
-            tri_made[r, :, :, span] = product.reshape(16, 8, LANES).astype(BF16)
+            tri_made[r, :, :, span] = moved.reshape(16, 8, LANES).astype(BF16)
         send_plane(r, tri_made, tri_mid, p_tri)
         return carry
 
@@ -338,30 +350,32 @@
         whole(tri_held.at[r], z_tri.at[r])
         for block in range(BLOCKS):
             span = pl.ds(block * LANES, LANES)
-            triangles = unweave(tri_held[r, :, span].astype(F32))
-            total, counted = 0.0, 0.0
-            for t in range(2):
-                tri_normed = norm(triangles[t], gains[1]).astype(BF16)
-                updated = pair[t, r, :, span].astype(F32) + gate[r, t, :, span] * dot(
-                    out_t[...], tri_normed
-                )
-                trans_in = norm(updated, gains[2]).astype(BF16)
-                hidden = jnp.maximum(dot(up_t[...], trans_in), 0.0).astype(BF16)
-                stacked = updated + dot(down_t[...], hidden)
-                final = norm(stacked, gains[3])
-                coverage = own_mask[r, t : t + 1, :] * template_mask[t : t + 1, span].astype(F32)
-                total = total + coverage * final
-                counted = counted + coverage
-            averaged = total / jnp.maximum(counted, 1.0)
-            activated = jnp.transpose(jnp.maximum(averaged, 0.0)).astype(BF16)
-            out_held[r, span, :] = dot(activated, embed_weight[...]).astype(BF16)
+            triangle = unweave(tri_held[r, :, span].astype(F32))
+            pairs = jnp.concatenate([pair[t, r, :, span].astype(F32) for t in range(2)], axis=0)
+            tri_normed = norm_both(triangle, gains[1]).astype(BF16)
+            updated = pairs + gate[r, :, span] * dot(out_t[...], tri_normed)
+            trans_in = norm_both(updated, gains[2]).astype(BF16)
+            hidden = jnp.maximum(dot(up_t[...], trans_in), 0.0).astype(BF16)
+            final = norm_both(updated + dot(down_t[...], hidden), gains[3])
+            coverage = own_mask[r] * template_mask[:, span].astype(F32)
+            total = coverage[0:1] * final[0:64] + coverage[1:2] * final[64:128]
+            averaged = total / jnp.maximum(coverage[0:1] + coverage[1:2], 1.0)
+            out_held[r, :, span] = jnp.maximum(averaged, 0.0).astype(BF16)
         pltpu.make_async_copy(out_held.at[r], result.at[r], result_sem.at[r]).start()
         return carry
 
     lax.fori_loop(0, ROWS, send_right, 0)
+
+    def send_left(r):
+        send_z(r, left_sent, left_mid, z_left)
 
     def right_step(r, carry):
         pass_right(r, 0)
+
+        @pl.when(r == ROWS - 1)
+        def _():
+            for first in range(AHEAD):
+                send_left(first)
 
         @pl.when(r > 0)
         def _():
@@ -369,27 +383,32 @@
 
         return carry
 
+    lax.fori_loop(0, BLOCKS, order, 0)
     lax.fori_loop(0, ROWS, right_step, 0)
     give_right(ROWS - 1, 0)
     pass_left(0, 0)
+    send_left(AHEAD)
     lax.fori_loop(0, ROWS, flatten, 0)
-    lax.fori_loop(0, BLOCKS, order, 0)
 
     def step(s, carry):
-        @pl.when(s < ROWS)
+        pass_left(s, 0)
+
+        @pl.when(s + AHEAD < ROWS)
         def _():
-            pass_left(s, 0)
+            send_left(s + AHEAD)
 
         multiply(s - 1, 0)
-
-        @pl.when(s > 1)
-        def _():
-            give_back(s - 2, 0)
-
-        return carry
-
-    lax.fori_loop(1, ROWS + 1, step, 0)
-    give_back(ROWS - 1, 0)
+        return carry
+
+    lax.fori_loop(1, ROWS - 1, step, 0)
+    give_back(0, 0)
+    pass_left(ROWS - 1, 0)
+    give_back(1, 0)
+    multiply(ROWS - 2, 0)
+    give_back(2, 0)
+    multiply(ROWS - 1, 0)
+    give_back(3, 0)
+    give_back(4, 0)
     lax.fori_loop(0, ROWS, finish, 0)
 
     def left_by_now(r, carry):
@@ -410,21 +429,21 @@
     blocks = (ROWS, 16, 8, L)
     dma = pltpu.SemaphoreType.DMA
     vmem = pltpu.VMEM
-    return pl.pallas_call(
+    activated = pl.pallas_call(
         kernel,
-        out_shape=jax.ShapeDtypeStruct((ROWS, L, 128), BF16),
-        in_specs=[pl.BlockSpec(memory_space=pltpu.VMEM)] * 13,
+        out_shape=jax.ShapeDtypeStruct((ROWS, 64, L), BF16),
+        in_specs=[pl.BlockSpec(memory_space=pltpu.VMEM)] * 12,
         out_specs=pl.BlockSpec(memory_space=pl.ANY),
         scratch_shapes=[
             vmem((320, 64), BF16),
-            vmem((64, 64), BF16),
-            vmem((128, 64), BF16),
-            vmem((64, 128), BF16),
+            vmem((128, 128), BF16),
+            vmem((256, 128), BF16),
+            vmem((128, 256), BF16),
             vmem((4, 64, 1), F32),
             vmem((ROWS, 2, 1), F32),
             vmem((128, 128), BF16),
             vmem((128, 128), BF16),
-            vmem((ROWS, 2, 64, L), F32),
+            vmem((ROWS, 128, L), F32),
             vmem(flat, BF16),
             vmem(flat, BF16),
             vmem(flat, BF16),
@@ -434,13 +453,14 @@
             vmem(blocks, BF16),
             vmem((2, *blocks), BF16),
             vmem((128, L), BF16),
+            vmem((128, L), BF16),
             vmem((L, L), BF16),
             vmem((L, L), BF16),
             vmem(blocks, BF16),
             vmem(blocks, BF16),
             vmem(flat, BF16),
             vmem(flat, BF16),
-            vmem((ROWS, L, 128), BF16),
+            vmem((ROWS, 64, L), BF16),
             *[dma((ROWS,)) for _ in range(7)],
             dma,
             dma,
@@ -461,10 +481,12 @@
         out_weight,
         trans_gain.reshape(1, -1),
         up_weight,
-        down_weight,
+        down_weight.T,
         final_gain.reshape(1, -1),
-        embed_weight,
     )
+    return jnp.einsum(
+        "rcl,cp->rlp", activated, embed_weight, preferred_element_type=F32
+    ).astype(BF16)
 
 
 def solution(mesh):

time: 150 us -> 126 us (0.84)
  Pallas kernels: 145 us -> 123 us
  local copies, waits for them, and re-layouts: 4.13 us -> 0.01 us
  matrix products: 0 us -> 2.96 us
    pallas_call x1, Pallas kernels: 145 us -> 123 us  [local(): pl.pallas_call(kernel, out_shape=jax.ShapeDtypeStruct((ROWS, 64, L), BF16...]
    unnamed x2, local copies, waits for them, and re-layouts: 4.13 us -> 0.01 us
    dot_general x0 -> x1, matrix products: none -> 2.96 us  [local(): jnp.einsum('rcl,cp->rlp', activated, embed_weight, preferred_element_type...]
where the time goes in v2:
time: 126 us
  Pallas kernels  123 us (98%)
  matrix products  2.96 us (2%)
    pallas_call x1, Pallas kernels, local(): pl.pallas_call(kernel, out_shape=jax.ShapeDtypeStruct((ROWS, 64, L), BF16...  123 us
    dot_general x1, matrix products, local(): jnp.einsum('rcl,cp->rlp', activated, embed_weight, preferred_element_type...  2.96 us

profile of v2, /device:TPU:1, one launch (start us, length us, event | category | flops | bytes accessed | tf_op | source)
XLA Modules:
  0.0 125.6 jit_solution(6541664032443447073)
XLA Ops:
  0.0 0.0 copy-start
  0.0 122.7 %shard_map.127 = bf16[5,64,1280]{2,1,0:T(8,128)(2,1)} custom-call(bf16[2,5,64,1280]{3,2,1,0:T(8,128)(2,1)} %bitcast.10, s32[5,1280]{1,0:T(8,128)} %pair_mask.1, s32[2,1280]{1,0:T(2,128)} %template_mask.1, f32[1,64]{1,0:T(1,128)} %bitcast.12, bf16[64,256]{1,0:T(8,128)(2,1)} %proj_weight.1, bf16[64,64]{1,0:T(8,128)(2,1)} %gate_weight.1, f32[1,64]{1,0:T(1,128)} %bitcast.13, ...), custom_call_target="tpu_custom_call" | custom-call | tf_op jit(solution)/shard_map/pallas_call | solution.py:432
  122.7 0.0 copy-done
  122.7 3.0 %convolution_convert_fusion = bf16[5,1280,128]{2,1,0:T(8,128)(2,1)} fusion(bf16[5,64,1280]{2,1,0:T(8,128)(2,1)} %shard_map.127, bf16[64,128]{1,0:T(8,128)(2,1)S(1)} %copy-done), kind=kOutput, calls=%fused_computation | convolution fusion | flops 105676800 | bytes 2473984 | tf_op jit(solution)/shard_map/rcl,cp->rlp/dot_general | solution.py:487
Async XLA Ops:
  0.0 122.7 %copy-start = (bf16[64,128]{1,0:T(8,128)(2,1)S(1)}, bf16[64,128]{1,0:T(8,128)(2,1)}, u32[]{:S(2)}) copy-start(bf16[64,128]{1,0:T(8,128)(2,1)} %param.25) | copy-start | bytes 49156

commit v3 on v2

--- a/solution.py
+++ b/solution.py
@@ -15,7 +15,7 @@
 L = 1280
 LANES = 256
 BLOCKS = L // LANES
-AHEAD = 2
+WIDE = 640
 
 
 def device_at(plane, z, core):
@@ -348,8 +348,8 @@
 
     def finish(r, carry):
         whole(tri_held.at[r], z_tri.at[r])
-        for block in range(BLOCKS):
-            span = pl.ds(block * LANES, LANES)
+        for block in range(L // WIDE):
+            span = pl.ds(block * WIDE, WIDE)
             triangle = unweave(tri_held[r, :, span].astype(F32))
             pairs = jnp.concatenate([pair[t, r, :, span].astype(F32) for t in range(2)], axis=0)
             tri_normed = norm_both(triangle, gains[1]).astype(BF16)
@@ -372,9 +372,9 @@
     def right_step(r, carry):
         pass_right(r, 0)
 
-        @pl.when(r == ROWS - 1)
+        @pl.when(r == 4)
         def _():
-            for first in range(AHEAD):
+            for first in [0]:
                 send_left(first)
 
         @pl.when(r > 0)
@@ -386,22 +386,21 @@
     lax.fori_loop(0, BLOCKS, order, 0)
     lax.fori_loop(0, ROWS, right_step, 0)
     give_right(ROWS - 1, 0)
+    send_left(1)
     pass_left(0, 0)
-    send_left(AHEAD)
+    send_left(2)
     lax.fori_loop(0, ROWS, flatten, 0)
 
     def step(s, carry):
         pass_left(s, 0)
-
-        @pl.when(s + AHEAD < ROWS)
-        def _():
-            send_left(s + AHEAD)
-
+        send_left(s + 2)
         multiply(s - 1, 0)
         return carry
 
-    lax.fori_loop(1, ROWS - 1, step, 0)
+    lax.fori_loop(1, ROWS - 2, step, 0)
+    pass_left(ROWS - 2, 0)
     give_back(0, 0)
+    multiply(ROWS - 3, 0)
     pass_left(ROWS - 1, 0)
     give_back(1, 0)
     multiply(ROWS - 2, 0)

time: 126 us -> 123 us (0.976)
  Pallas kernels: 123 us -> 120 us
    pallas_call x1, Pallas kernels: 123 us -> 120 us  [local(): pl.pallas_call(kernel, out_shape=jax.ShapeDtypeStruct((ROWS, 64, L), BF16...]
where the time goes in v3:
time: 123 us; the launch traced here: 122 us
  Pallas kernels  120 us (98%)
  matrix products  2.95 us (2%)
    pallas_call x1, Pallas kernels, local(): pl.pallas_call(kernel, out_shape=jax.ShapeDtypeStruct((ROWS, 64, L), BF16...  120 us
    dot_general x1, matrix products, local(): jnp.einsum('rcl,cp->rlp', activated, embed_weight, preferred_element_type...  2.95 us

profile of v3, /device:TPU:1, one launch (start us, length us, event | category | flops | bytes accessed | tf_op | source)
XLA Modules:
  0.0 122.5 jit_solution(44556261214755438)
XLA Ops:
  0.0 0.0 copy-start
  0.0 119.5 %shard_map.127 = bf16[5,64,1280]{2,1,0:T(8,128)(2,1)} custom-call(bf16[2,5,64,1280]{3,2,1,0:T(8,128)(2,1)} %bitcast.10, s32[5,1280]{1,0:T(8,128)} %pair_mask.1, s32[2,1280]{1,0:T(2,128)} %template_mask.1, f32[1,64]{1,0:T(1,128)} %bitcast.12, bf16[64,256]{1,0:T(8,128)(2,1)} %proj_weight.1, bf16[64,64]{1,0:T(8,128)(2,1)} %gate_weight.1, f32[1,64]{1,0:T(1,128)} %bitcast.13, ...), custom_call_target="tpu_custom_call" | custom-call | tf_op jit(solution)/shard_map/pallas_call | solution.py:431
  119.5 0.0 copy-done
  119.5 3.0 %convolution_convert_fusion = bf16[5,1280,128]{2,1,0:T(8,128)(2,1)} fusion(bf16[5,64,1280]{2,1,0:T(8,128)(2,1)} %shard_map.127, bf16[64,128]{1,0:T(8,128)(2,1)S(1)} %copy-done), kind=kOutput, calls=%fused_computation | convolution fusion | flops 105676800 | bytes 2473984 | tf_op jit(solution)/shard_map/rcl,cp->rlp/dot_general | solution.py:486
Async XLA Ops:
  0.0 119.5 %copy-start = (bf16[64,128]{1,0:T(8,128)(2,1)S(1)}, bf16[64,128]{1,0:T(8,128)(2,1)}, u32[]{:S(2)}) copy-start(bf16[64,128]{1,0:T(8,128)(2,1)} %param.25) | copy-start | bytes 49156

commit v4 on v3

--- a/solution.py
+++ b/solution.py
@@ -16,6 +16,7 @@
 LANES = 256
 BLOCKS = L // LANES
 WIDE = 640
+HALVES = L // WIDE
 
 
 def device_at(plane, z, core):
@@ -55,6 +56,10 @@
     blocks = both.shape[0] // 8
     pieces = [both[8 * b : 8 * b + 8] for t in range(2) for b in range(t, blocks, 2)]
     return jnp.concatenate(pieces, axis=0)
+
+
+def columns(half):
+    return pl.ds(half * WIDE if isinstance(half, int) else pl.multiple_of(half * WIDE, 128), WIDE)
 
 
 def whole(ref, sem):
@@ -180,13 +185,13 @@
             left_sent[r, :, span] = weave(*lefts).astype(BF16)
             gate[r, :, span] = jnp.concatenate(gates, axis=0)
 
-    def send_z(r, sent, mid, recv):
+    def send_z(r, sent, mid, recv, span=pl.ds(0, L)):
         def send(g, slot, where):
             pltpu.make_async_remote_copy(
-                sent.at[r, pl.ds(pl.multiple_of(g * 16, 16), 16)],
-                mid.at[r, pl.ds(pl.multiple_of(slot * 16, 16), 16)],
+                sent.at[r, pl.ds(pl.multiple_of(g * 16, 16), 16), span],
+                mid.at[r, pl.ds(pl.multiple_of(slot * 16, 16), 16), span],
                 z_out,
-                recv.at[r],
+                recv,
                 device_id=where,
                 device_id_type=MESH,
             ).start()
@@ -196,46 +201,44 @@
             send((z + 7 - m) & (Z - 1), m * 2 + core, device_at(place, z - m, 1))
         send((z + 7 + core) & (Z - 1), 6 * core + core, device_at(place, z, 1 - core))
         pltpu.make_async_copy(
-            sent.at[r, pl.ds(pl.multiple_of(group * 16, 16), 16)],
-            mid.at[r, pl.ds(pl.multiple_of((6 - 5 * core) * 16, 16), 16)],
-            recv.at[r],
+            sent.at[r, pl.ds(pl.multiple_of(group * 16, 16), 16), span],
+            mid.at[r, pl.ds(pl.multiple_of((6 - 5 * core) * 16, 16), 16), span],
+            recv,
         ).start()
 
-    def send_plane(r, turned, held, recv):
+    def send_plane(r, turned, held, recv, span=pl.ds(0, L)):
         def send(step, carry):
             other = lax.bitwise_xor(place, step)
             pltpu.make_async_remote_copy(
-                turned.at[r, other],
-                held.at[r, place],
+                turned.at[r, other, :, span],
+                held.at[r, place, :, span],
                 p_out,
-                recv.at[r],
+                recv,
                 device_id=device_at(other, z, core),
                 device_id_type=MESH,
             ).start()
             return carry
 
         lax.fori_loop(1, 16, send, 0)
-        pltpu.make_async_copy(turned.at[r, place], held.at[r, place], recv.at[r]).start()
-
-    def turn(r, mid, turned):
-        for block in range(BLOCKS):
-            span = pl.ds(block * LANES, LANES)
-            moved = dot(forth[...], mid[r, :, span])
-            turned[r, :, :, span] = moved.reshape(16, 8, LANES).astype(BF16)
-
-    def turn_back(r):
-        for block in range(BLOCKS):
-            span = pl.ds(block * LANES, LANES)
-            value = tri_mid[r, :, :, span].astype(F32).reshape(128, LANES).astype(BF16)
-            tri_turned[r, :, span] = dot(back[...], value).astype(BF16)
-
-    def send_back(r):
+        pltpu.make_async_copy(
+            turned.at[r, place, :, span], held.at[r, place, :, span], recv
+        ).start()
+
+    def turn(r, mid, turned, span):
+        moved = dot(forth[...], mid[r, :, span])
+        turned[r, :, :, span] = moved.reshape(16, 8, -1).astype(BF16)
+
+    def turn_back(r, span):
+        value = tri_mid[r, :, :, span].astype(F32).reshape(128, -1).astype(BF16)
+        tri_turned[r, :, span] = dot(back[...], value).astype(BF16)
+
+    def send_back(r, span, recv):
         def send(slot, where):
             pltpu.make_async_remote_copy(
-                tri_turned.at[r, pl.ds(pl.multiple_of(slot * 16, 16), 16)],
-                tri_held.at[r, pl.ds(pl.multiple_of(group * 16, 16), 16)],
+                tri_turned.at[r, pl.ds(pl.multiple_of(slot * 16, 16), 16), span],
+                tri_held.at[r, pl.ds(pl.multiple_of(group * 16, 16), 16), span],
                 z_out,
-                z_tri.at[r],
+                recv,
                 device_id=where,
                 device_id_type=MESH,
             ).start()
@@ -246,9 +249,9 @@
                 send(slot, device_at(place, z - m + 2 * m * core, other))
         send(7 - 7 * core, device_at(place, z, 1 - core))
         pltpu.make_async_copy(
-            tri_turned.at[r, pl.ds(pl.multiple_of((6 - 5 * core) * 16, 16), 16)],
-            tri_held.at[r, pl.ds(pl.multiple_of(group * 16, 16), 16)],
-            z_tri.at[r],
+            tri_turned.at[r, pl.ds(pl.multiple_of((6 - 5 * core) * 16, 16), 16), span],
+            tri_held.at[r, pl.ds(pl.multiple_of(group * 16, 16), 16), span],
+            recv,
         ).start()
 
     def exchange(r):
@@ -268,13 +271,14 @@
         def _():
             pl.semaphore_wait(barrier, 30)
 
-        send_z(r, right_sent, right_mid, z_right)
+        send_z(r, right_sent, right_mid, z_right.at[r])
         return carry
 
     def pass_right(r, carry):
         whole(right_mid.at[r], z_right.at[r])
-        turn(r, right_mid, right_turned)
-        send_plane(r, right_turned, right_held.at[core], p_right)
+        for half in range(HALVES):
+            turn(r, right_mid, right_turned, columns(half))
+        send_plane(r, right_turned, right_held.at[core], p_right.at[r])
         return carry
 
     def give_right(r, carry):
@@ -283,9 +287,11 @@
         return carry
 
     def pass_left(r, carry):
-        whole(left_mid.at[r], z_left.at[r])
-        turn(r, left_mid, left_turned)
-        send_plane(r, left_turned, left_held, p_left)
+        for half in range(HALVES):
+            span = columns(half)
+            whole(left_mid.at[r, :, span], z_left.at[r, half])
+            turn(r, left_mid, left_turned, span)
+            send_plane(r, left_turned, left_held, p_left.at[r], span)
         return carry
 
     def flatten(r, carry):
@@ -328,28 +334,30 @@
                 preferred_element_type=F32,
             )
             tri_flat[:, span] = product.astype(BF16)
-        for block in range(BLOCKS):
-            span = pl.ds(block * LANES, LANES)
+        for half in range(HALVES):
+            span = columns(half)
             moved = lax.dot_general(
                 tri_flat[...],
                 right_rows[span, :],
                 (((1,), (1,)), ((), ())),
                 preferred_element_type=F32,
             )
-            tri_made[r, :, :, span] = moved.reshape(16, 8, LANES).astype(BF16)
-        send_plane(r, tri_made, tri_mid, p_tri)
+            tri_made[r, :, :, span] = moved.reshape(16, 8, WIDE).astype(BF16)
+            send_plane(r, tri_made, tri_mid, p_tri.at[r, half], span)
         return carry
 
     def give_back(r, carry):
-        whole(tri_mid.at[r], p_tri.at[r])
-        turn_back(r)
-        send_back(r)
+        for half in range(HALVES):
+            span = columns(half)
+            whole(tri_mid.at[r, :, :, span], p_tri.at[r, half])
+            turn_back(r, span)
+            send_back(r, span, z_tri.at[r, half])
         return carry
 
     def finish(r, carry):
-        whole(tri_held.at[r], z_tri.at[r])
-        for block in range(L // WIDE):
-            span = pl.ds(block * WIDE, WIDE)
+        for half in range(HALVES):
+            span = columns(half)
+            whole(tri_held.at[r, :, span], z_tri.at[r, half])
             triangle = unweave(tri_held[r, :, span].astype(F32))
             pairs = jnp.concatenate([pair[t, r, :, span].astype(F32) for t in range(2)], axis=0)
             tri_normed = norm_both(triangle, gains[1]).astype(BF16)
@@ -361,13 +369,16 @@
             total = coverage[0:1] * final[0:64] + coverage[1:2] * final[64:128]
             averaged = total / jnp.maximum(coverage[0:1] + coverage[1:2], 1.0)
             out_held[r, :, span] = jnp.maximum(averaged, 0.0).astype(BF16)
-        pltpu.make_async_copy(out_held.at[r], result.at[r], result_sem.at[r]).start()
+            pltpu.make_async_copy(
+                out_held.at[r, :, span], result.at[r, :, span], result_sem.at[r]
+            ).start()
         return carry
 
     lax.fori_loop(0, ROWS, send_right, 0)
 
     def send_left(r):
-        send_z(r, left_sent, left_mid, z_left)
+        for half in range(HALVES):
+            send_z(r, left_sent, left_mid, z_left.at[r, half], columns(half))
 
     def right_step(r, carry):
         pass_right(r, 0)
@@ -460,7 +471,8 @@
             vmem(flat, BF16),
             vmem(flat, BF16),
             vmem((ROWS, 64, L), BF16),
-            *[dma((ROWS,)) for _ in range(7)],
+            *[dma((ROWS, HALVES)), dma((ROWS,)), dma((ROWS, HALVES))],
+            *[dma((ROWS,)), dma((ROWS,)), dma((ROWS, HALVES)), dma((ROWS,))],
             dma,
             dma,
             dma,

time: 123 us -> 121 us (0.984)
  Pallas kernels: 120 us -> 117 us
    pallas_call x1, Pallas kernels: 120 us -> 117 us  [local(): pl.pallas_call(kernel, out_shape=jax.ShapeDtypeStruct((ROWS, 64, L), BF16...]
where the time goes in v4:
time: 121 us; the launch traced here: 120 us
  Pallas kernels  117 us (97%)
  matrix products  2.95 us (2%)
    pallas_call x1, Pallas kernels, local(): pl.pallas_call(kernel, out_shape=jax.ShapeDtypeStruct((ROWS, 64, L), BF16...  117 us
    dot_general x1, matrix products, local(): jnp.einsum('rcl,cp->rlp', activated, embed_weight, preferred_element_type...  2.95 us

profile of v4, /device:TPU:1, one launch (start us, length us, event | category | flops | bytes accessed | tf_op | source)
XLA Modules:
  0.0 120.5 jit_solution(15849687028973832089)
XLA Ops:
  0.0 0.0 copy-start
  0.0 117.5 %shard_map.127 = bf16[5,64,1280]{2,1,0:T(8,128)(2,1)} custom-call(bf16[2,5,64,1280]{3,2,1,0:T(8,128)(2,1)} %bitcast.10, s32[5,1280]{1,0:T(8,128)} %pair_mask.1, s32[2,1280]{1,0:T(2,128)} %template_mask.1, f32[1,64]{1,0:T(1,128)} %bitcast.12, bf16[64,256]{1,0:T(8,128)(2,1)} %proj_weight.1, bf16[64,64]{1,0:T(8,128)(2,1)} %gate_weight.1, f32[1,64]{1,0:T(1,128)} %bitcast.13, ...), custom_call_target="tpu_custom_call" | custom-call | tf_op jit(solution)/shard_map/pallas_call | solution.py:442
  117.5 0.0 copy-done
  117.5 3.0 %convolution_convert_fusion = bf16[5,1280,128]{2,1,0:T(8,128)(2,1)} fusion(bf16[5,64,1280]{2,1,0:T(8,128)(2,1)} %shard_map.127, bf16[64,128]{1,0:T(8,128)(2,1)S(1)} %copy-done), kind=kOutput, calls=%fused_computation | convolution fusion | flops 105676800 | bytes 2473984 | tf_op jit(solution)/shard_map/rcl,cp->rlp/dot_general | solution.py:498
Async XLA Ops:
  0.0 117.5 %copy-start = (bf16[64,128]{1,0:T(8,128)(2,1)S(1)}, bf16[64,128]{1,0:T(8,128)(2,1)}, u32[]{:S(2)}) copy-start(bf16[64,128]{1,0:T(8,128)(2,1)} %param.25) | copy-start | bytes 49156

commit v5 on v4

--- a/solution.py
+++ b/solution.py
@@ -67,7 +67,7 @@
 
 
 def kernel(
-    pair,
+    pair_given,
     pair_mask,
     template_mask,
     in_gain,
@@ -80,6 +80,7 @@
     down_weight,
     final_gain,
     result,
+    pair,
     proj_t,
     out_t,
     up_t,
@@ -117,6 +118,7 @@
     p_out,
     across_out,
     result_sem,
+    pair_sem,
 ):
     row, col = lax.axis_index("row"), lax.axis_index("col")
     z, core = row & (Z - 1), col & 1
@@ -124,6 +126,12 @@
     device = row * 16 + col
     group = (z - core) & (Z - 1)
     partner = device_at(place, z + 1 - 2 * core, 1 - core)
+
+    def load(r):
+        return pltpu.make_async_copy(pair_given.at[:, r], pair.at[:, r], pair_sem.at[r])
+
+    for r in range(ROWS):
+        load(r).start()
 
     barrier = pltpu.get_barrier_semaphore()
     for step in range(1, Z):
@@ -148,29 +156,10 @@
 
     proj_t[0:256, :] = jnp.transpose(proj_weight[...].astype(F32)).astype(BF16)
     proj_t[256:320, :] = jnp.transpose(gate_weight[...].astype(F32)).astype(BF16)
-    out_t[...] = jnp.zeros_like(out_t)
-    up_t[...] = jnp.zeros_like(up_t)
-    down_t[...] = jnp.zeros_like(down_t)
-    for t in range(2):
-        own, wide = pl.ds(64 * t, 64), pl.ds(128 * t, 128)
-        out_t[own, own] = jnp.transpose(out_weight[...].astype(F32)).astype(BF16)
-        up_t[wide, own] = jnp.transpose(up_weight[...].astype(F32)).astype(BF16)
-        down_t[own, wide] = down_weight[...]
-    for n, vector in enumerate((in_gain, mid_gain, trans_gain, final_gain)):
-        gains[n] = column(vector[...])
-    lanes = lax.broadcasted_iota(jnp.int32, (2, L), 1)
-    for r in range(ROWS):
-        own_mask[r] = jnp.sum(
-            jnp.where(lanes == device * ROWS + r, template_mask[...].astype(F32), 0.0),
-            axis=1,
-            keepdims=True,
-        )
-    at = lax.broadcasted_iota(jnp.int32, (128, 128), 0)
-    of = lax.broadcasted_iota(jnp.int32, (128, 128), 1)
-    forth[...] = jnp.where(of == (at % 8) * 16 + at // 8, 1.0, 0.0).astype(BF16)
-    back[...] = jnp.where(of == (at % 16) * 8 + at // 16, 1.0, 0.0).astype(BF16)
+    gains[0] = column(in_gain[...])
 
     def make(r):
+        load(r).wait()
         for block in range(BLOCKS):
             span = pl.ds(block * LANES, LANES)
             mask = pair_mask[pl.ds(r, 1), span].astype(F32)
@@ -383,10 +372,9 @@
     def right_step(r, carry):
         pass_right(r, 0)
 
-        @pl.when(r == 4)
+        @pl.when(r == ROWS - 1)
         def _():
-            for first in [0]:
-                send_left(first)
+            send_left(0)
 
         @pl.when(r > 0)
         def _():
@@ -394,6 +382,27 @@
 
         return carry
 
+    out_t[...] = jnp.zeros_like(out_t)
+    up_t[...] = jnp.zeros_like(up_t)
+    down_t[...] = jnp.zeros_like(down_t)
+    for t in range(2):
+        own, wide = pl.ds(64 * t, 64), pl.ds(128 * t, 128)
+        out_t[own, own] = jnp.transpose(out_weight[...].astype(F32)).astype(BF16)
+        up_t[wide, own] = jnp.transpose(up_weight[...].astype(F32)).astype(BF16)
+        down_t[own, wide] = down_weight[...]
+    for n, vector in enumerate((mid_gain, trans_gain, final_gain)):
+        gains[n + 1] = column(vector[...])
+    lanes = lax.broadcasted_iota(jnp.int32, (2, L), 1)
+    for r in range(ROWS):
+        own_mask[r] = jnp.sum(
+            jnp.where(lanes == device * ROWS + r, template_mask[...].astype(F32), 0.0),
+            axis=1,
+            keepdims=True,
+        )
+    at = lax.broadcasted_iota(jnp.int32, (128, 128), 0)
+    of = lax.broadcasted_iota(jnp.int32, (128, 128), 1)
+    forth[...] = jnp.where(of == (at % 8) * 16 + at // 8, 1.0, 0.0).astype(BF16)
+    back[...] = jnp.where(of == (at % 16) * 8 + at // 16, 1.0, 0.0).astype(BF16)
     lax.fori_loop(0, BLOCKS, order, 0)
     lax.fori_loop(0, ROWS, right_step, 0)
     give_right(ROWS - 1, 0)
@@ -442,9 +451,13 @@
     activated = pl.pallas_call(
         kernel,
         out_shape=jax.ShapeDtypeStruct((ROWS, 64, L), BF16),
-        in_specs=[pl.BlockSpec(memory_space=pltpu.VMEM)] * 12,
+        in_specs=[
+            pl.BlockSpec(memory_space=pl.ANY),
+            *[pl.BlockSpec(memory_space=pltpu.VMEM)] * 11,
+        ],
         out_specs=pl.BlockSpec(memory_space=pl.ANY),
         scratch_shapes=[
+            vmem((2, ROWS, 64, L), BF16),
             vmem((320, 64), BF16),
             vmem((128, 128), BF16),
             vmem((256, 128), BF16),
@@ -477,6 +490,7 @@
             dma,
             dma,
             dma((ROWS,)),
+            dma((ROWS,)),
         ],
         compiler_params=pltpu.CompilerParams(
             collective_id=0, has_side_effects=True, vmem_limit_bytes=60 * 2**20

time: 121 us -> 120 us (level)
  no operation moved by 1% of the time
where the time goes in v5:
time: 120 us
  Pallas kernels  117 us (98%)
  matrix products  2.96 us (2%)
    pallas_call x1, Pallas kernels, local(): pl.pallas_call(kernel, out_shape=jax.ShapeDtypeStruct((ROWS, 64, L), BF16...  117 us
    dot_general x1, matrix products, local(): jnp.einsum('rcl,cp->rlp', activated, embed_weight, preferred_element_type...  2.96 us

profile of v5, /device:TPU:1, one launch (start us, length us, event | category | flops | bytes accessed | tf_op | source)
XLA Modules:
  0.0 119.8 jit_solution(13802183780519388505)
XLA Ops:
  0.0 0.0 copy-start
  0.0 116.8 %shard_map.127 = bf16[5,64,1280]{2,1,0:T(8,128)(2,1)} custom-call(bf16[2,5,64,1280]{3,2,1,0:T(8,128)(2,1)} %bitcast.10, s32[5,1280]{1,0:T(8,128)} %pair_mask.1, s32[2,1280]{1,0:T(2,128)} %template_mask.1, f32[1,64]{1,0:T(1,128)} %bitcast.12, bf16[64,256]{1,0:T(8,128)(2,1)} %proj_weight.1, bf16[64,64]{1,0:T(8,128)(2,1)} %gate_weight.1, f32[1,64]{1,0:T(1,128)} %bitcast.13, ...), custom_call_target="tpu_custom_call" | custom-call | tf_op jit(solution)/shard_map/pallas_call | solution.py:451
  116.8 0.0 copy-done
  116.8 3.0 %convolution_convert_fusion = bf16[5,1280,128]{2,1,0:T(8,128)(2,1)} fusion(bf16[5,64,1280]{2,1,0:T(8,128)(2,1)} %shard_map.127, bf16[64,128]{1,0:T(8,128)(2,1)S(1)} %copy-done), kind=kOutput, calls=%fused_computation | convolution fusion | flops 105676800 | bytes 2473984 | tf_op jit(solution)/shard_map/rcl,cp->rlp/dot_general | solution.py:512
Async XLA Ops:
  0.0 116.8 %copy-start = (bf16[64,128]{1,0:T(8,128)(2,1)S(1)}, bf16[64,128]{1,0:T(8,128)(2,1)}, u32[]{:S(2)}) copy-start(bf16[64,128]{1,0:T(8,128)(2,1)} %param.25) | copy-start | bytes 49156

commit v6 on v5

--- a/solution.py
+++ b/solution.py
@@ -100,6 +100,7 @@
     right_held,
     left_flat,
     tri_flat,
+    tri_part,
     right_flat,
     right_rows,
     tri_made,
@@ -280,7 +281,7 @@
             span = columns(half)
             whole(left_mid.at[r, :, span], z_left.at[r, half])
             turn(r, left_mid, left_turned, span)
-            send_plane(r, left_turned, left_held, p_left.at[r], span)
+            send_plane(r, left_turned, left_held, p_left.at[r, half], span)
         return carry
 
     def flatten(r, carry):
@@ -309,20 +310,23 @@
         return carry
 
     def multiply(r, carry):
-        whole(left_held.at[r], p_left.at[r])
-        for block in range(BLOCKS):
-            span = pl.ds(block * LANES, LANES)
-            value = left_held[r, :, :, span].astype(F32).reshape(128, LANES)
+        for half in range(HALVES):
+            span = columns(half)
+            whole(left_held.at[r, :, :, span], p_left.at[r, half])
+            value = left_held[r, :, :, span].astype(F32).reshape(128, WIDE)
             left_flat[:, span] = value.astype(BF16)
-        for block in range(BLOCKS):
-            span = pl.ds(block * LANES, LANES)
-            product = lax.dot_general(
-                left_flat[...],
-                right_flat[span, :],
-                (((1,), (1,)), ((), ())),
-                preferred_element_type=F32,
-            )
-            tri_flat[:, span] = product.astype(BF16)
+            for block in range(BLOCKS):
+                rows = pl.ds(block * LANES, LANES)
+                product = lax.dot_general(
+                    left_flat[:, span],
+                    right_flat[rows, span],
+                    (((1,), (1,)), ((), ())),
+                    preferred_element_type=F32,
+                )
+                if half == 0:
+                    tri_part[:, rows] = product
+                else:
+                    tri_flat[:, rows] = (tri_part[:, rows] + product).astype(BF16)
         for half in range(HALVES):
             span = columns(half)
             moved = lax.dot_general(
@@ -477,6 +481,7 @@
             vmem((2, *blocks), BF16),
             vmem((128, L), BF16),
             vmem((128, L), BF16),
+            vmem((128, L), F32),
             vmem((L, L), BF16),
             vmem((L, L), BF16),
             vmem(blocks, BF16),
@@ -485,7 +490,7 @@
             vmem(flat, BF16),
             vmem((ROWS, 64, L), BF16),
             *[dma((ROWS, HALVES)), dma((ROWS,)), dma((ROWS, HALVES))],
-            *[dma((ROWS,)), dma((ROWS,)), dma((ROWS, HALVES)), dma((ROWS,))],
+            *[dma((ROWS, HALVES)), dma((ROWS,)), dma((ROWS, HALVES)), dma((ROWS,))],
             dma,
             dma,
             dma,

time: 120 us -> 120 us (level)
  no operation moved by 1% of the time
where the time goes in v6:
time: 120 us
  Pallas kernels  117 us (98%)
  matrix products  2.96 us (2%)
    pallas_call x1, Pallas kernels, local(): pl.pallas_call(kernel, out_shape=jax.ShapeDtypeStruct((ROWS, 64, L), BF16...  117 us
    dot_general x1, matrix products, local(): jnp.einsum('rcl,cp->rlp', activated, embed_weight, preferred_element_type...  2.96 us

profile of v6, /device:TPU:1, one launch (start us, length us, event | category | flops | bytes accessed | tf_op | source)
XLA Modules:
  0.0 119.5 jit_solution(4737913064423650685)
XLA Ops:
  0.0 0.0 copy-start
  0.0 116.6 %shard_map.127 = bf16[5,64,1280]{2,1,0:T(8,128)(2,1)} custom-call(bf16[2,5,64,1280]{3,2,1,0:T(8,128)(2,1)} %bitcast.10, s32[5,1280]{1,0:T(8,128)} %pair_mask.1, s32[2,1280]{1,0:T(2,128)} %template_mask.1, f32[1,64]{1,0:T(1,128)} %bitcast.12, bf16[64,256]{1,0:T(8,128)(2,1)} %proj_weight.1, bf16[64,64]{1,0:T(8,128)(2,1)} %gate_weight.1, f32[1,64]{1,0:T(1,128)} %bitcast.13, ...), custom_call_target="tpu_custom_call" | custom-call | tf_op jit(solution)/shard_map/pallas_call | solution.py:455
  116.6 0.0 copy-done
  116.6 3.0 %convolution_convert_fusion = bf16[5,1280,128]{2,1,0:T(8,128)(2,1)} fusion(bf16[5,64,1280]{2,1,0:T(8,128)(2,1)} %shard_map.127, bf16[64,128]{1,0:T(8,128)(2,1)S(1)} %copy-done), kind=kOutput, calls=%fused_computation | convolution fusion | flops 105676800 | bytes 2473984 | tf_op jit(solution)/shard_map/rcl,cp->rlp/dot_general | solution.py:517
Async XLA Ops:
  0.0 116.6 %copy-start = (bf16[64,128]{1,0:T(8,128)(2,1)S(1)}, bf16[64,128]{1,0:T(8,128)(2,1)}, u32[]{:S(2)}) copy-start(bf16[64,128]{1,0:T(8,128)(2,1)} %param.25) | copy-start | bytes 49156
